TPU v7x, 512 devices: a whole 4x8x8 slice. The times are simulated.
512 devices in a mesh: group: 16 (over y, core), member: 32 (over x, z).
Axes of the slice: x: 4, y: 8, z: 8, core: 2. Of those that a mesh axis runs over, the one named last changes fastest.
Arguments:
- heads: bfloat16 [1048576, 768], P(('group', 'member')), may hold values from -16 to 16
- new_heads: bfloat16 [1024, 768], P('group'), may hold values from -16 to 16
- vectors: bfloat16 [512, 128, 768], P(('group', 'member')), may hold values from -16 to 16
- near_ids: int32 [512, 64], P(('group', 'member')), may hold values from 0 to 65535, as said below
Outputs:
- density: float32 [1024], P('group')
- spread: float32 [1024], P('group')
- reassign: float32 [512, 64, 128], P(('group', 'member'))
Inputs may be any that keep to these rules, and one draw needn't show every extreme that they name: `near_ids`: each row holds 64 different numbers; of one row at most 4 lie in one range j * 2048 to (j + 1) * 2048 - 1, and exactly 4 in some such range.
All inputs are finite; a program needn't handle non-finite values.
Results may differ from a plain program's by a relative error of at most 0.0003.
Values may be sent and summed in bfloat16 or wider, within the bound.
A program may use at most 64 MiB of HBM per device.

v0:
```python
import jax
import jax.numpy as jnp
from jax import lax
from jax.sharding import PartitionSpec as P


def passed_along(value, axis, steps):
    count = lax.axis_size(axis)
    pairs = [(source, (source + steps) % count) for source in range(count)]
    return lax.ppermute(value, axis, pairs)


def crowding(block, heads, head_sq, width):
    query_sq = jnp.sum(jnp.square(block.astype(jnp.float32)), axis=1)
    dots = lax.dot_general(
        block, heads, (((1,), (1,)), ((), ())), preferred_element_type=jnp.float32
    )
    excess = (query_sq[:, None] + head_sq[None, :] - 2.0 * dots) / width
    weight = 1.0 / jnp.square(1.0 + excess)
    return jnp.stack([jnp.sum(weight, axis=1), jnp.sum(weight * excess, axis=1)])


def distances(vec, rows, width):
    vec_sq = jnp.sum(jnp.square(vec.astype(jnp.float32)), axis=2)
    row_sq = jnp.sum(jnp.square(rows.astype(jnp.float32)), axis=2)
    dots = jnp.einsum("pbd,pkd->pkb", vec, rows, preferred_element_type=jnp.float32)
    return (row_sq[:, :, None] + vec_sq[:, None, :] - 2.0 * dots) / width


def per_device(heads, new_heads, vectors, near_ids):
    head_dev = heads.shape[0]
    width = heads.shape[1]
    groups = lax.axis_size("group")
    members = lax.axis_size("member")
    here = lax.axis_index("group")
    me = lax.axis_index("member")
    head_sq = jnp.sum(jnp.square(heads.astype(jnp.float32)), axis=1)
    new_count = new_heads.shape[0]
    table = jnp.zeros((groups, 2, new_count), jnp.float32)
    table = lax.dynamic_update_slice(
        table, crowding(new_heads, heads, head_sq, width)[None], (here, 0, 0)
    )

    def advance(step, carry):
        block, sums = carry
        block = passed_along(block, "group", 1)
        anchor = (here - step) % groups
        sums = lax.dynamic_update_slice(
            sums, crowding(block, heads, head_sq, width)[None], (anchor, 0, 0)
        )
        return (block, sums)

    unused, table = lax.fori_loop(1, groups, advance, (new_heads, table))
    mine = lax.psum_scatter(table, "group", scatter_dimension=0, tiled=True)
    mine = lax.psum(mine, "member")
    total_heads = float(head_dev * groups * members)
    density = jnp.log(mine[0, 0] / total_heads)
    spread = mine[0, 1] / mine[0, 0]
    lists = lax.all_gather(near_ids, "member", axis=0, tiled=True)
    blocks = lax.all_gather(vectors, "member", axis=0, tiled=True)
    owner = lists // head_dev
    local = lists % head_dev
    rows = jnp.take(heads, local, axis=0)
    rows, owned = (rows, owner == me)
    reassign = lax.psum_scatter(
        jnp.where(owned[:, :, None], distances(blocks, rows, width), 0.0),
        "member",
        scatter_dimension=0,
        tiled=True,
    )
    return (density, spread, reassign)


def solution(mesh):
    placed = (
        P(("group", "member"), None),
        P("group", None),
        P(("group", "member"), None, None),
        P(("group", "member"), None),
    )
    return jax.shard_map(
        per_device,
        mesh=mesh,
        in_specs=placed,
        out_specs=(P("group"), P("group"), P(("group", "member"), None, None)),
        check_vma=False,
    )
```

profile of v0, /device:TPU:32, one launch (start us, length us, event | category | flops | bytes accessed | tf_op | source)
XLA Modules:
  0.0 345.6 jit_solution(508991916548334194)
XLA Ops:
  8.2 44.1 %all-gather = s32[32,1,64]{2,1,0:T(1,128)S(1)} all-gather(s32[1,1,64]{2,1,0:T(1,128)} %bitcast.40), channel_id=1, replica_groups=mesh['group'=16,'member'=32] {'member'}, dimensions={0}, use_global_device_ids=true | all-gather | bytes 8448 | tf_op jit(solution)/shard_map/all_gather | solution.py:59
  53.8 12.6 %gather_fusion = bf16[2048,768]{1,0:T(8,128)(2,1)} fusion(bf16[2048,768]{1,0:T(8,128)(2,1)} %param.6, s32[2048]{0:T(1024)S(1)} %broadcast_clamp_fusion), kind=kCustom, calls=%fused_computation | custom fusion | bytes 6299648 | tf_op jit(solution)/shard_map/jit(_take)/gather | solution.py:63
  69.0 1.3 multiply_reduce_fusion.3
  70.4 39.8 %all-gather.3.cloned.1.call-done = bf16[32,128,768]{2,1,0:T(8,128)(2,1)} async-done(((bf16[1,128,768]{2,1,0:T(8,128)(2,1)}), bf16[32,128,768]{2,1,0:T(8,128)(2,1)}) %all-gather.3.cloned.1.call-update) | async-done | bytes 6291472 | tf_op jit(solution)/shard_map/all_gather | solution.py:60
  110.2 4.2 %multiply_reduce_fusion.2 = f32[32,128]{1,0:T(8,128)S(1)} fusion(bf16[32,128,768]{2,1,0:T(8,128)(2,1)} %all-gather.3.cloned.1.call-done), kind=kLoop, calls=%fused_computation.9 | loop fusion | flops 9433088 | bytes 6307840 | tf_op jit(solution)/shard_map/reduce_sum | solution.py:24
  114.4 5.3 %fusion.9 = f32[32,64,128]{2,1,0:T(8,128)} fusion(bf16[32,128,768]{2,1,0:T(8,128)(2,1)} %all-gather.3.cloned.1.call-done, bf16[32,64,768]{2,1,0:T(8,128)(2,1)S(1)} %bitcast.36, pred[32,64]{1,0:T(8,128)(4,1)S(1)} %get-tuple-element.175, f32[32,128]{1,0:T(8,128)S(1)} %multiply_reduce_fusion.2, f32[32,64]{1,0:T(8,128)S(1)} %multiply_reduce_fusion.3, ...), kind=kOutput, calls=%fused_computation.21 | convolution fusion | flops 405536768 | bytes 10514432 | tf_op jit(solution)/shard_map/pbd,pkd->pkb/dot_general | solution.py:26
  119.8 99.5 %while.17 = (s32[]{:T(128)}, bf16[64,768]{1,0:T(8,128)(2,1)S(1)}, f32[16,2,64]{2,1,0:T(2,128)S(1)}, f32[2048]{0:T(1024)S(1)}, bf16[2048,768]{1,0:T(8,128)(2,1)S(...) while((s32[]{:T(128)}, bf16[64,768]{1,0:T(8,128)(2,1)S(1)}, ...), condition=%wide.region_8.9_spmd, body=%wide.region_4.8_spmd.sunk | while | flops 202784720 | bytes 3943724 | solution.py:53
  119.8 5.2 %collective-permute-done = bf16[64,768]{1,0:T(8,128)(2,1)S(1)} collective-permute-done((bf16[64,768]{1,0:T(8,128)(2,1)S(1)}, bf16[64,768]{1,0:T(8,128)(2,1)S(1)}, u32[]{:S(2)}, u32[]{:S(2)}) %collective-permute-start) | collective-permute-done | bytes 98336 | tf_op jit(solution)/shard_map/while/body/eval_jaxpr/ppermute | solution.py:10
  126.4 5.2 %collective-permute-done = bf16[64,768]{1,0:T(8,128)(2,1)S(1)} collective-permute-done((bf16[64,768]{1,0:T(8,128)(2,1)S(1)}, bf16[64,768]{1,0:T(8,128)(2,1)S(1)}, u32[]{:S(2)}, u32[]{:S(2)}) %collective-permute-start) | collective-permute-done | bytes 98336 | tf_op jit(solution)/shard_map/while/body/eval_jaxpr/ppermute | solution.py:10
  133.1 5.2 %collective-permute-done = bf16[64,768]{1,0:T(8,128)(2,1)S(1)} collective-permute-done((bf16[64,768]{1,0:T(8,128)(2,1)S(1)}, bf16[64,768]{1,0:T(8,128)(2,1)S(1)}, u32[]{:S(2)}, u32[]{:S(2)}) %collective-permute-start) | collective-permute-done | bytes 98336 | tf_op jit(solution)/shard_map/while/body/eval_jaxpr/ppermute | solution.py:10
  139.7 5.2 %collective-permute-done = bf16[64,768]{1,0:T(8,128)(2,1)S(1)} collective-permute-done((bf16[64,768]{1,0:T(8,128)(2,1)S(1)}, bf16[64,768]{1,0:T(8,128)(2,1)S(1)}, u32[]{:S(2)}, u32[]{:S(2)}) %collective-permute-start) | collective-permute-done | bytes 98336 | tf_op jit(solution)/shard_map/while/body/eval_jaxpr/ppermute | solution.py:10
  146.3 5.2 %collective-permute-done = bf16[64,768]{1,0:T(8,128)(2,1)S(1)} collective-permute-done((bf16[64,768]{1,0:T(8,128)(2,1)S(1)}, bf16[64,768]{1,0:T(8,128)(2,1)S(1)}, u32[]{:S(2)}, u32[]{:S(2)}) %collective-permute-start) | collective-permute-done | bytes 98336 | tf_op jit(solution)/shard_map/while/body/eval_jaxpr/ppermute | solution.py:10
  153.0 5.2 %collective-permute-done = bf16[64,768]{1,0:T(8,128)(2,1)S(1)} collective-permute-done((bf16[64,768]{1,0:T(8,128)(2,1)S(1)}, bf16[64,768]{1,0:T(8,128)(2,1)S(1)}, u32[]{:S(2)}, u32[]{:S(2)}) %collective-permute-start) | collective-permute-done | bytes 98336 | tf_op jit(solution)/shard_map/while/body/eval_jaxpr/ppermute | solution.py:10
  159.6 5.2 %collective-permute-done = bf16[64,768]{1,0:T(8,128)(2,1)S(1)} collective-permute-done((bf16[64,768]{1,0:T(8,128)(2,1)S(1)}, bf16[64,768]{1,0:T(8,128)(2,1)S(1)}, u32[]{:S(2)}, u32[]{:S(2)}) %collective-permute-start) | collective-permute-done | bytes 98336 | tf_op jit(solution)/shard_map/while/body/eval_jaxpr/ppermute | solution.py:10
  166.2 5.2 %collective-permute-done = bf16[64,768]{1,0:T(8,128)(2,1)S(1)} collective-permute-done((bf16[64,768]{1,0:T(8,128)(2,1)S(1)}, bf16[64,768]{1,0:T(8,128)(2,1)S(1)}, u32[]{:S(2)}, u32[]{:S(2)}) %collective-permute-start) | collective-permute-done | bytes 98336 | tf_op jit(solution)/shard_map/while/body/eval_jaxpr/ppermute | solution.py:10
  172.9 5.2 %collective-permute-done = bf16[64,768]{1,0:T(8,128)(2,1)S(1)} collective-permute-done((bf16[64,768]{1,0:T(8,128)(2,1)S(1)}, bf16[64,768]{1,0:T(8,128)(2,1)S(1)}, u32[]{:S(2)}, u32[]{:S(2)}) %collective-permute-start) | collective-permute-done | bytes 98336 | tf_op jit(solution)/shard_map/while/body/eval_jaxpr/ppermute | solution.py:10
  179.5 5.2 %collective-permute-done = bf16[64,768]{1,0:T(8,128)(2,1)S(1)} collective-permute-done((bf16[64,768]{1,0:T(8,128)(2,1)S(1)}, bf16[64,768]{1,0:T(8,128)(2,1)S(1)}, u32[]{:S(2)}, u32[]{:S(2)}) %collective-permute-start) | collective-permute-done | bytes 98336 | tf_op jit(solution)/shard_map/while/body/eval_jaxpr/ppermute | solution.py:10
  186.1 5.2 %collective-permute-done = bf16[64,768]{1,0:T(8,128)(2,1)S(1)} collective-permute-done((bf16[64,768]{1,0:T(8,128)(2,1)S(1)}, bf16[64,768]{1,0:T(8,128)(2,1)S(1)}, u32[]{:S(2)}, u32[]{:S(2)}) %collective-permute-start) | collective-permute-done | bytes 98336 | tf_op jit(solution)/shard_map/while/body/eval_jaxpr/ppermute | solution.py:10
  192.8 5.2 %collective-permute-done = bf16[64,768]{1,0:T(8,128)(2,1)S(1)} collective-permute-done((bf16[64,768]{1,0:T(8,128)(2,1)S(1)}, bf16[64,768]{1,0:T(8,128)(2,1)S(1)}, u32[]{:S(2)}, u32[]{:S(2)}) %collective-permute-start) | collective-permute-done | bytes 98336 | tf_op jit(solution)/shard_map/while/body/eval_jaxpr/ppermute | solution.py:10
  199.4 5.2 %collective-permute-done = bf16[64,768]{1,0:T(8,128)(2,1)S(1)} collective-permute-done((bf16[64,768]{1,0:T(8,128)(2,1)S(1)}, bf16[64,768]{1,0:T(8,128)(2,1)S(1)}, u32[]{:S(2)}, u32[]{:S(2)}) %collective-permute-start) | collective-permute-done | bytes 98336 | tf_op jit(solution)/shard_map/while/body/eval_jaxpr/ppermute | solution.py:10
  206.0 5.2 %collective-permute-done = bf16[64,768]{1,0:T(8,128)(2,1)S(1)} collective-permute-done((bf16[64,768]{1,0:T(8,128)(2,1)S(1)}, bf16[64,768]{1,0:T(8,128)(2,1)S(1)}, u32[]{:S(2)}, u32[]{:S(2)}) %collective-permute-start) | collective-permute-done | bytes 98336 | tf_op jit(solution)/shard_map/while/body/eval_jaxpr/ppermute | solution.py:10
  212.7 5.2 %collective-permute-done = bf16[64,768]{1,0:T(8,128)(2,1)S(1)} collective-permute-done((bf16[64,768]{1,0:T(8,128)(2,1)S(1)}, bf16[64,768]{1,0:T(8,128)(2,1)S(1)}, u32[]{:S(2)}, u32[]{:S(2)}) %collective-permute-start) | collective-permute-done | bytes 98336 | tf_op jit(solution)/shard_map/while/body/eval_jaxpr/ppermute | solution.py:10
  219.3 46.5 %all-reduce = f32[16,2,64]{2,1,0:T(2,128)S(1)} all-reduce(f32[16,2,64]{2,1,0:T(2,128)S(1)} %get-tuple-element.158), channel_id=2, replica_groups=mesh['group'=16,'member'=32] {'group'}, use_global_device_ids=true, to_apply=%region_9.10.clone | all-reduce | flops 2048 | bytes 16384
  266.4 71.8 %psum.7 = f32[1,2,64]{2,1,0:T(2,128)S(1)} all-reduce(f32[1,2,64]{2,1,0:T(2,128)S(1)} %constant_dynamic-slice_fusion), channel_id=1, replica_groups=mesh['group'=16,'member'=32] {'member'}, use_global_device_ids=true, to_apply=%region_10.11 | all-reduce | flops 128 | bytes 1024 | tf_op jit(solution)/shard_map/psum | solution.py:55
  (98 shorter events, 26.7 us)
Async XLA Ops:
  7.2 103.0 %all-gather.3.cloned.1.call-start = ((), (), s32[]{:S(2)}) async-start(), calls=%async_computation.1 | async-start | bytes 6488064 | tf_op jit(solution)/shard_map/all_gather | solution.py:60
  8.1 330.6 %reduce-scatter.2.cloned.1.call-start = ((), (), s32[]{:S(2)}) async-start(), calls=%async_computation.2 | async-start | bytes 1081344 | tf_op jit(solution)/shard_map/reduce_scatter | solution.py:65
  53.8 12.7 %copy-start = (bf16[2048,768]{1,0:T(8,128)(2,1)S(1)}, bf16[2048,768]{1,0:T(8,128)(2,1)}, u32[]{:S(2)}) copy-start(bf16[2048,768]{1,0:T(8,128)(2,1)} %param.6) | copy-start | bytes 9437188
  67.1 1.9 copy-start.1
  110.2 4.2 %copy-start.2 = (bf16[2048,768]{1,0:T(8,128)(2,1)S(1)}, bf16[2048,768]{1,0:T(8,128)(2,1)}, u32[]{:S(2)}) copy-start(bf16[2048,768]{1,0:T(8,128)(2,1)} %gather_fusion) | copy-start | bytes 9437188
  119.8 5.3 %collective-permute-start = (bf16[64,768]{1,0:T(8,128)(2,1)S(1)}, bf16[64,768]{1,0:T(8,128)(2,1)S(1)}, u32[]{:S(2)}, u32[]{:S(2)}) collective-permute-start(bf16[64,768]{1,0:T(8,128)(2,1)S(1)} %get-tuple-element.232), channel_id=1, source_target_pairs={{0,32},{32,64},{64,96},{96,128},{128,160},{160,192},{192,224},{224... | collective-permute-start | bytes 294920 | tf_op jit(solution)/shard_map/while/body/eval_jaxpr/ppermute | solution.py:10
  126.4 5.3 %collective-permute-start = (bf16[64,768]{1,0:T(8,128)(2,1)S(1)}, bf16[64,768]{1,0:T(8,128)(2,1)S(1)}, u32[]{:S(2)}, u32[]{:S(2)}) collective-permute-start(bf16[64,768]{1,0:T(8,128)(2,1)S(1)} %get-tuple-element.232), channel_id=1, source_target_pairs={{0,32},{32,64},{64,96},{96,128},{128,160},{160,192},{192,224},{224... | collective-permute-start | bytes 294920 | tf_op jit(solution)/shard_map/while/body/eval_jaxpr/ppermute | solution.py:10
  133.0 5.3 %collective-permute-start = (bf16[64,768]{1,0:T(8,128)(2,1)S(1)}, bf16[64,768]{1,0:T(8,128)(2,1)S(1)}, u32[]{:S(2)}, u32[]{:S(2)}) collective-permute-start(bf16[64,768]{1,0:T(8,128)(2,1)S(1)} %get-tuple-element.232), channel_id=1, source_target_pairs={{0,32},{32,64},{64,96},{96,128},{128,160},{160,192},{192,224},{224... | collective-permute-start | bytes 294920 | tf_op jit(solution)/shard_map/while/body/eval_jaxpr/ppermute | solution.py:10
  139.7 5.3 %collective-permute-start = (bf16[64,768]{1,0:T(8,128)(2,1)S(1)}, bf16[64,768]{1,0:T(8,128)(2,1)S(1)}, u32[]{:S(2)}, u32[]{:S(2)}) collective-permute-start(bf16[64,768]{1,0:T(8,128)(2,1)S(1)} %get-tuple-element.232), channel_id=1, source_target_pairs={{0,32},{32,64},{64,96},{96,128},{128,160},{160,192},{192,224},{224... | collective-permute-start | bytes 294920 | tf_op jit(solution)/shard_map/while/body/eval_jaxpr/ppermute | solution.py:10
  146.3 5.3 %collective-permute-start = (bf16[64,768]{1,0:T(8,128)(2,1)S(1)}, bf16[64,768]{1,0:T(8,128)(2,1)S(1)}, u32[]{:S(2)}, u32[]{:S(2)}) collective-permute-start(bf16[64,768]{1,0:T(8,128)(2,1)S(1)} %get-tuple-element.232), channel_id=1, source_target_pairs={{0,32},{32,64},{64,96},{96,128},{128,160},{160,192},{192,224},{224... | collective-permute-start | bytes 294920 | tf_op jit(solution)/shard_map/while/body/eval_jaxpr/ppermute | solution.py:10
  152.9 5.3 %collective-permute-start = (bf16[64,768]{1,0:T(8,128)(2,1)S(1)}, bf16[64,768]{1,0:T(8,128)(2,1)S(1)}, u32[]{:S(2)}, u32[]{:S(2)}) collective-permute-start(bf16[64,768]{1,0:T(8,128)(2,1)S(1)} %get-tuple-element.232), channel_id=1, source_target_pairs={{0,32},{32,64},{64,96},{96,128},{128,160},{160,192},{192,224},{224... | collective-permute-start | bytes 294920 | tf_op jit(solution)/shard_map/while/body/eval_jaxpr/ppermute | solution.py:10
  159.6 5.3 %collective-permute-start = (bf16[64,768]{1,0:T(8,128)(2,1)S(1)}, bf16[64,768]{1,0:T(8,128)(2,1)S(1)}, u32[]{:S(2)}, u32[]{:S(2)}) collective-permute-start(bf16[64,768]{1,0:T(8,128)(2,1)S(1)} %get-tuple-element.232), channel_id=1, source_target_pairs={{0,32},{32,64},{64,96},{96,128},{128,160},{160,192},{192,224},{224... | collective-permute-start | bytes 294920 | tf_op jit(solution)/shard_map/while/body/eval_jaxpr/ppermute | solution.py:10
  166.2 5.3 %collective-permute-start = (bf16[64,768]{1,0:T(8,128)(2,1)S(1)}, bf16[64,768]{1,0:T(8,128)(2,1)S(1)}, u32[]{:S(2)}, u32[]{:S(2)}) collective-permute-start(bf16[64,768]{1,0:T(8,128)(2,1)S(1)} %get-tuple-element.232), channel_id=1, source_target_pairs={{0,32},{32,64},{64,96},{96,128},{128,160},{160,192},{192,224},{224... | collective-permute-start | bytes 294920 | tf_op jit(solution)/shard_map/while/body/eval_jaxpr/ppermute | solution.py:10
  172.8 5.3 %collective-permute-start = (bf16[64,768]{1,0:T(8,128)(2,1)S(1)}, bf16[64,768]{1,0:T(8,128)(2,1)S(1)}, u32[]{:S(2)}, u32[]{:S(2)}) collective-permute-start(bf16[64,768]{1,0:T(8,128)(2,1)S(1)} %get-tuple-element.232), channel_id=1, source_target_pairs={{0,32},{32,64},{64,96},{96,128},{128,160},{160,192},{192,224},{224... | collective-permute-start | bytes 294920 | tf_op jit(solution)/shard_map/while/body/eval_jaxpr/ppermute | solution.py:10
  179.5 5.3 %collective-permute-start = (bf16[64,768]{1,0:T(8,128)(2,1)S(1)}, bf16[64,768]{1,0:T(8,128)(2,1)S(1)}, u32[]{:S(2)}, u32[]{:S(2)}) collective-permute-start(bf16[64,768]{1,0:T(8,128)(2,1)S(1)} %get-tuple-element.232), channel_id=1, source_target_pairs={{0,32},{32,64},{64,96},{96,128},{128,160},{160,192},{192,224},{224... | collective-permute-start | bytes 294920 | tf_op jit(solution)/shard_map/while/body/eval_jaxpr/ppermute | solution.py:10
  186.1 5.3 %collective-permute-start = (bf16[64,768]{1,0:T(8,128)(2,1)S(1)}, bf16[64,768]{1,0:T(8,128)(2,1)S(1)}, u32[]{:S(2)}, u32[]{:S(2)}) collective-permute-start(bf16[64,768]{1,0:T(8,128)(2,1)S(1)} %get-tuple-element.232), channel_id=1, source_target_pairs={{0,32},{32,64},{64,96},{96,128},{128,160},{160,192},{192,224},{224... | collective-permute-start | bytes 294920 | tf_op jit(solution)/shard_map/while/body/eval_jaxpr/ppermute | solution.py:10
  192.7 5.3 %collective-permute-start = (bf16[64,768]{1,0:T(8,128)(2,1)S(1)}, bf16[64,768]{1,0:T(8,128)(2,1)S(1)}, u32[]{:S(2)}, u32[]{:S(2)}) collective-permute-start(bf16[64,768]{1,0:T(8,128)(2,1)S(1)} %get-tuple-element.232), channel_id=1, source_target_pairs={{0,32},{32,64},{64,96},{96,128},{128,160},{160,192},{192,224},{224... | collective-permute-start | bytes 294920 | tf_op jit(solution)/shard_map/while/body/eval_jaxpr/ppermute | solution.py:10
  199.4 5.3 %collective-permute-start = (bf16[64,768]{1,0:T(8,128)(2,1)S(1)}, bf16[64,768]{1,0:T(8,128)(2,1)S(1)}, u32[]{:S(2)}, u32[]{:S(2)}) collective-permute-start(bf16[64,768]{1,0:T(8,128)(2,1)S(1)} %get-tuple-element.232), channel_id=1, source_target_pairs={{0,32},{32,64},{64,96},{96,128},{128,160},{160,192},{192,224},{224... | collective-permute-start | bytes 294920 | tf_op jit(solution)/shard_map/while/body/eval_jaxpr/ppermute | solution.py:10
  206.0 5.3 %collective-permute-start = (bf16[64,768]{1,0:T(8,128)(2,1)S(1)}, bf16[64,768]{1,0:T(8,128)(2,1)S(1)}, u32[]{:S(2)}, u32[]{:S(2)}) collective-permute-start(bf16[64,768]{1,0:T(8,128)(2,1)S(1)} %get-tuple-element.232), channel_id=1, source_target_pairs={{0,32},{32,64},{64,96},{96,128},{128,160},{160,192},{192,224},{224... | collective-permute-start | bytes 294920 | tf_op jit(solution)/shard_map/while/body/eval_jaxpr/ppermute | solution.py:10
  212.6 5.3 %collective-permute-start = (bf16[64,768]{1,0:T(8,128)(2,1)S(1)}, bf16[64,768]{1,0:T(8,128)(2,1)S(1)}, u32[]{:S(2)}, u32[]{:S(2)}) collective-permute-start(bf16[64,768]{1,0:T(8,128)(2,1)S(1)} %get-tuple-element.232), channel_id=1, source_target_pairs={{0,32},{32,64},{64,96},{96,128},{128,160},{160,192},{192,224},{224... | collective-permute-start | bytes 294920 | tf_op jit(solution)/shard_map/while/body/eval_jaxpr/ppermute | solution.py:10
Sparse Core Ops, SparseCore 0:
  11.2 98.9 all-gather.2
  119.9 217.1 reduce-scatter.1
where the time goes:
time: 346 us
  blocking collectives  162 us (47%)
  waiting for transfers between devices  118 us (34%)
  matrix products  24.4 us (7%)
  local copies, waits for them, and re-layouts  16.3 us (5%)
  between operations  14.1 us (4%)
  other arithmetic  9.04 us (3%)
    ppermute x15, waiting for transfers between devices, passed_along(): return lax.ppermute(value, axis, pairs)  78.2 us
    psum x1, blocking collectives, per_device(): mine = lax.psum(mine, 'member')  71.8 us
    unnamed x1, blocking collectives  46.5 us
    all_gather x1, blocking collectives, per_device(): lists = lax.all_gather(near_ids, 'member', axis=0, tiled=True)  44.1 us
    all_gather x1, waiting for transfers between devices, per_device(): blocks = lax.all_gather(vectors, 'member', axis=0, tiled=True)  39.8 us
    dot_general x16, matrix products, crowding(): lax.dot_general(block, heads, (((1,), (1,)), ((), ())), preferred_element...  19.2 us
    gather x1, local copies, waits for them, and re-layouts, per_device(): rows = jnp.take(heads, local, axis=0)  12.6 us
  transfers between devices with their start and end apart: 17, of which 16 were waited for; matrix products, arithmetic and copies ran while one was open for 11% of the time, Pallas kernels for 0%

commit v1 on v0

--- a/solution.py
+++ b/solution.py
@@ -52,7 +52,12 @@
 
     unused, table = lax.fori_loop(1, groups, advance, (new_heads, table))
     mine = lax.psum_scatter(table, "group", scatter_dimension=0, tiled=True)
-    mine = lax.psum(mine, "member")
+    size = lax.axis_size("member")
+    result, hop = (mine, 1)
+    while hop < size:
+        result = result + lax.ppermute(result, "member", [(i, i ^ hop) for i in range(size)])
+        hop = 2 * hop
+    mine = result
     total_heads = float(head_dev * groups * members)
     density = jnp.log(mine[0, 0] / total_heads)
     spread = mine[0, 1] / mine[0, 0]

time: 346 us -> 345 us (level)
  the two profiles are of different devices: /device:TPU:32 before, /device:TPU:8 now
where the time goes in v1:
time: 345 us; the launch traced here: 344 us
  waiting for transfers between devices  169 us (49%)
  blocking collectives  94.2 us (27%)
  matrix products  24.4 us (7%)
  local copies, waits for them, and re-layouts  16.3 us (5%)
  starting transfers between devices  15.5 us (4%)
  between operations  14.2 us (4%)
  other arithmetic  9.68 us (3%)
    ppermute x15, waiting for transfers between devices, passed_along(): return lax.ppermute(value, axis, pairs)  71.5 us
    unnamed x1, blocking collectives  50 us
    all_gather x1, blocking collectives, per_device(): lists = lax.all_gather(near_ids, 'member', axis=0, tiled=True)  44.2 us
    all_gather x1, waiting for transfers between devices, per_device(): blocks = lax.all_gather(vectors, 'member', axis=0, tiled=True)  40.1 us
    reduce_scatter x1, waiting for transfers between devices, per_device(): lax.psum_scatter(jnp.where(owned[:, :, None], distances(blocks, rows, wid...  39.2 us
    dot_general x16, matrix products, crowding(): lax.dot_general(block, heads, (((1,), (1,)), ((), ())), preferred_element...  19.1 us
    ppermute x5, waiting for transfers between devices, per_device(): lax.ppermute(result, 'member', [(i, i ^ hop) for i in range(size)])  18.4 us
    ppermute x5, starting transfers between devices, per_device(): lax.ppermute(result, 'member', [(i, i ^ hop) for i in range(size)])  15.2 us
  transfers between devices with their start and end apart: 22, of which 22 were waited for; matrix products, arithmetic and copies ran while one was open for 11% of the time, Pallas kernels for 0%

profile of v1, /device:TPU:8, one launch (start us, length us, event | category | flops | bytes accessed | tf_op | source)
XLA Modules:
  0.0 344.2 jit_solution(3698289854586114317)
XLA Ops:
  8.2 44.2 %all-gather = s32[32,1,64]{2,1,0:T(1,128)S(1)} all-gather(s32[1,1,64]{2,1,0:T(1,128)} %bitcast.40), channel_id=1, replica_groups=mesh['group'=16,'member'=32] {'member'}, dimensions={0}, use_global_device_ids=true | all-gather | bytes 8448 | tf_op jit(solution)/shard_map/all_gather | solution.py:64
  53.8 12.6 %gather_fusion = bf16[2048,768]{1,0:T(8,128)(2,1)} fusion(bf16[2048,768]{1,0:T(8,128)(2,1)} %param.6, s32[2048]{0:T(1024)S(1)} %broadcast_clamp_fusion), kind=kCustom, calls=%fused_computation | custom fusion | bytes 6299648 | tf_op jit(solution)/shard_map/jit(_take)/gather | solution.py:68
  70.4 40.1 %all-gather.3.cloned.1.call-done = bf16[32,128,768]{2,1,0:T(8,128)(2,1)} async-done(((bf16[1,128,768]{2,1,0:T(8,128)(2,1)}), bf16[32,128,768]{2,1,0:T(8,128)(2,1)}) %all-gather.3.cloned.1.call-update) | async-done | bytes 6291472 | tf_op jit(solution)/shard_map/all_gather | solution.py:65
  110.5 4.2 %multiply_reduce_fusion.2 = f32[32,128]{1,0:T(8,128)S(1)} fusion(bf16[32,128,768]{2,1,0:T(8,128)(2,1)} %all-gather.3.cloned.1.call-done), kind=kLoop, calls=%fused_computation.9 | loop fusion | flops 9433088 | bytes 6307840 | tf_op jit(solution)/shard_map/reduce_sum | solution.py:24
  114.7 5.3 %fusion.9 = f32[32,64,128]{2,1,0:T(8,128)} fusion(bf16[32,128,768]{2,1,0:T(8,128)(2,1)} %all-gather.3.cloned.1.call-done, bf16[32,64,768]{2,1,0:T(8,128)(2,1)S(1)} %bitcast.36, pred[32,64]{1,0:T(8,128)(4,1)S(1)} %get-tuple-element.175, f32[32,128]{1,0:T(8,128)S(1)} %multiply_reduce_fusion.2, f32[32,64]{1,0:T(8,128)S(1)} %multiply_reduce_fusion.3, ...), kind=kOutput, calls=%fused_computation.21 | convolution fusion | flops 405536768 | bytes 10514432 | tf_op jit(solution)/shard_map/pbd,pkd->pkb/dot_general | solution.py:26
  120.0 92.7 %while.17 = (s32[]{:T(128)}, bf16[64,768]{1,0:T(8,128)(2,1)S(1)}, f32[16,2,64]{2,1,0:T(2,128)S(1)}, f32[2048]{0:T(1024)S(1)}, bf16[2048,768]{1,0:T(8,128)(2,1)S(...) while((s32[]{:T(128)}, bf16[64,768]{1,0:T(8,128)(2,1)S(1)}, ...), condition=%wide.region_8.9_spmd, body=%wide.region_4.8_spmd.sunk | while | flops 202784720 | bytes 3943724 | solution.py:53
  120.1 4.0 %collective-permute-done = bf16[64,768]{1,0:T(8,128)(2,1)S(1)} collective-permute-done((bf16[64,768]{1,0:T(8,128)(2,1)S(1)}, bf16[64,768]{1,0:T(8,128)(2,1)S(1)}, u32[]{:S(2)}, u32[]{:S(2)}) %collective-permute-start) | collective-permute-done | bytes 98336 | tf_op jit(solution)/shard_map/while/body/eval_jaxpr/ppermute | solution.py:10
  125.5 4.0 %collective-permute-done = bf16[64,768]{1,0:T(8,128)(2,1)S(1)} collective-permute-done((bf16[64,768]{1,0:T(8,128)(2,1)S(1)}, bf16[64,768]{1,0:T(8,128)(2,1)S(1)}, u32[]{:S(2)}, u32[]{:S(2)}) %collective-permute-start) | collective-permute-done | bytes 98336 | tf_op jit(solution)/shard_map/while/body/eval_jaxpr/ppermute | solution.py:10
  130.9 4.0 %collective-permute-done = bf16[64,768]{1,0:T(8,128)(2,1)S(1)} collective-permute-done((bf16[64,768]{1,0:T(8,128)(2,1)S(1)}, bf16[64,768]{1,0:T(8,128)(2,1)S(1)}, u32[]{:S(2)}, u32[]{:S(2)}) %collective-permute-start) | collective-permute-done | bytes 98336 | tf_op jit(solution)/shard_map/while/body/eval_jaxpr/ppermute | solution.py:10
  141.8 4.0 %collective-permute-done = bf16[64,768]{1,0:T(8,128)(2,1)S(1)} collective-permute-done((bf16[64,768]{1,0:T(8,128)(2,1)S(1)}, bf16[64,768]{1,0:T(8,128)(2,1)S(1)}, u32[]{:S(2)}, u32[]{:S(2)}) %collective-permute-start) | collective-permute-done | bytes 98336 | tf_op jit(solution)/shard_map/while/body/eval_jaxpr/ppermute | solution.py:10
  147.2 4.5 %collective-permute-done = bf16[64,768]{1,0:T(8,128)(2,1)S(1)} collective-permute-done((bf16[64,768]{1,0:T(8,128)(2,1)S(1)}, bf16[64,768]{1,0:T(8,128)(2,1)S(1)}, u32[]{:S(2)}, u32[]{:S(2)}) %collective-permute-start) | collective-permute-done | bytes 98336 | tf_op jit(solution)/shard_map/while/body/eval_jaxpr/ppermute | solution.py:10
  153.1 5.2 %collective-permute-done = bf16[64,768]{1,0:T(8,128)(2,1)S(1)} collective-permute-done((bf16[64,768]{1,0:T(8,128)(2,1)S(1)}, bf16[64,768]{1,0:T(8,128)(2,1)S(1)}, u32[]{:S(2)}, u32[]{:S(2)}) %collective-permute-start) | collective-permute-done | bytes 98336 | tf_op jit(solution)/shard_map/while/body/eval_jaxpr/ppermute | solution.py:10
  159.8 5.2 %collective-permute-done = bf16[64,768]{1,0:T(8,128)(2,1)S(1)} collective-permute-done((bf16[64,768]{1,0:T(8,128)(2,1)S(1)}, bf16[64,768]{1,0:T(8,128)(2,1)S(1)}, u32[]{:S(2)}, u32[]{:S(2)}) %collective-permute-start) | collective-permute-done | bytes 98336 | tf_op jit(solution)/shard_map/while/body/eval_jaxpr/ppermute | solution.py:10
  166.4 5.2 %collective-permute-done = bf16[64,768]{1,0:T(8,128)(2,1)S(1)} collective-permute-done((bf16[64,768]{1,0:T(8,128)(2,1)S(1)}, bf16[64,768]{1,0:T(8,128)(2,1)S(1)}, u32[]{:S(2)}, u32[]{:S(2)}) %collective-permute-start) | collective-permute-done | bytes 98336 | tf_op jit(solution)/shard_map/while/body/eval_jaxpr/ppermute | solution.py:10
  173.0 5.2 %collective-permute-done = bf16[64,768]{1,0:T(8,128)(2,1)S(1)} collective-permute-done((bf16[64,768]{1,0:T(8,128)(2,1)S(1)}, bf16[64,768]{1,0:T(8,128)(2,1)S(1)}, u32[]{:S(2)}, u32[]{:S(2)}) %collective-permute-start) | collective-permute-done | bytes 98336 | tf_op jit(solution)/shard_map/while/body/eval_jaxpr/ppermute | solution.py:10
  179.7 5.2 %collective-permute-done = bf16[64,768]{1,0:T(8,128)(2,1)S(1)} collective-permute-done((bf16[64,768]{1,0:T(8,128)(2,1)S(1)}, bf16[64,768]{1,0:T(8,128)(2,1)S(1)}, u32[]{:S(2)}, u32[]{:S(2)}) %collective-permute-start) | collective-permute-done | bytes 98336 | tf_op jit(solution)/shard_map/while/body/eval_jaxpr/ppermute | solution.py:10
  186.3 5.2 %collective-permute-done = bf16[64,768]{1,0:T(8,128)(2,1)S(1)} collective-permute-done((bf16[64,768]{1,0:T(8,128)(2,1)S(1)}, bf16[64,768]{1,0:T(8,128)(2,1)S(1)}, u32[]{:S(2)}, u32[]{:S(2)}) %collective-permute-start) | collective-permute-done | bytes 98336 | tf_op jit(solution)/shard_map/while/body/eval_jaxpr/ppermute | solution.py:10
  192.9 5.2 %collective-permute-done = bf16[64,768]{1,0:T(8,128)(2,1)S(1)} collective-permute-done((bf16[64,768]{1,0:T(8,128)(2,1)S(1)}, bf16[64,768]{1,0:T(8,128)(2,1)S(1)}, u32[]{:S(2)}, u32[]{:S(2)}) %collective-permute-start) | collective-permute-done | bytes 98336 | tf_op jit(solution)/shard_map/while/body/eval_jaxpr/ppermute | solution.py:10
  199.6 5.2 %collective-permute-done = bf16[64,768]{1,0:T(8,128)(2,1)S(1)} collective-permute-done((bf16[64,768]{1,0:T(8,128)(2,1)S(1)}, bf16[64,768]{1,0:T(8,128)(2,1)S(1)}, u32[]{:S(2)}, u32[]{:S(2)}) %collective-permute-start) | collective-permute-done | bytes 98336 | tf_op jit(solution)/shard_map/while/body/eval_jaxpr/ppermute | solution.py:10
  206.2 5.2 %collective-permute-done = bf16[64,768]{1,0:T(8,128)(2,1)S(1)} collective-permute-done((bf16[64,768]{1,0:T(8,128)(2,1)S(1)}, bf16[64,768]{1,0:T(8,128)(2,1)S(1)}, u32[]{:S(2)}, u32[]{:S(2)}) %collective-permute-start) | collective-permute-done | bytes 98336 | tf_op jit(solution)/shard_map/while/body/eval_jaxpr/ppermute | solution.py:10
  212.8 50.0 %all-reduce = f32[16,2,64]{2,1,0:T(2,128)S(1)} all-reduce(f32[16,2,64]{2,1,0:T(2,128)S(1)} %get-tuple-element.158), channel_id=2, replica_groups=mesh['group'=16,'member'=32] {'group'}, use_global_device_ids=true, to_apply=%region_9.10.clone | all-reduce | flops 2048 | bytes 16384
  275.9 4.3 %collective-permute-start.3 = (f32[1,2,64]{2,1,0:T(2,128)S(1)}, f32[1,2,64]{2,1,0:T(2,128)S(1)}, u32[]{:S(2)}, u32[]{:S(2)}) collective-permute-start(f32[1,2,64]{2,1,0:T(2,128)S(1)} %add.163), channel_id=1, source_target_pairs={{0,4},{1,5},{2,6},{3,7},{4,0},{5,1},{6,2},{7,3},{8,12},{9,13},{10,... | collective-permute-start | bytes 1544 | tf_op jit(solution)/shard_map/ppermute | solution.py:58
  280.2 5.0 %collective-permute-done.3 = f32[1,2,64]{2,1,0:T(2,128)S(1)} collective-permute-done((f32[1,2,64]{2,1,0:T(2,128)S(1)}, f32[1,2,64]{2,1,0:T(2,128)S(1)}, u32[]{:S(2)}, u32[]{:S(2)}) %collective-permute-start.3) | collective-permute-done | bytes 544 | tf_op jit(solution)/shard_map/ppermute | solution.py:58
  298.2 39.2 %reduce-scatter.2.cloned.1.call-done = f32[1,64,128]{2,1,0:T(8,128)} async-done(((f32[32,64,128]{2,1,0:T(8,128)}), f32[1,64,128]{2,1,0:T(8,128)}) %reduce-scatter.2.cloned.1.call-update) | async-done | bytes 32784 | tf_op jit(solution)/shard_map/reduce_scatter | solution.py:70
  (112 shorter events, 56.9 us)
Async XLA Ops:
  7.2 103.3 %all-gather.3.cloned.1.call-start = ((), (), s32[]{:S(2)}) async-start(), calls=%async_computation.1 | async-start | bytes 6488064 | tf_op jit(solution)/shard_map/all_gather | solution.py:65
  8.1 329.2 %reduce-scatter.2.cloned.1.call-start = ((), (), s32[]{:S(2)}) async-start(), calls=%async_computation.2 | async-start | bytes 1081344 | tf_op jit(solution)/shard_map/reduce_scatter | solution.py:70
  53.8 12.7 %copy-start = (bf16[2048,768]{1,0:T(8,128)(2,1)S(1)}, bf16[2048,768]{1,0:T(8,128)(2,1)}, u32[]{:S(2)}) copy-start(bf16[2048,768]{1,0:T(8,128)(2,1)} %param.6) | copy-start | bytes 9437188
  110.5 4.2 %copy-start.2 = (bf16[2048,768]{1,0:T(8,128)(2,1)S(1)}, bf16[2048,768]{1,0:T(8,128)(2,1)}, u32[]{:S(2)}) copy-start(bf16[2048,768]{1,0:T(8,128)(2,1)} %gather_fusion) | copy-start | bytes 9437188
  120.0 4.1 %collective-permute-start = (bf16[64,768]{1,0:T(8,128)(2,1)S(1)}, bf16[64,768]{1,0:T(8,128)(2,1)S(1)}, u32[]{:S(2)}, u32[]{:S(2)}) collective-permute-start(bf16[64,768]{1,0:T(8,128)(2,1)S(1)} %get-tuple-element.232), channel_id=1, source_target_pairs={{0,32},{32,64},{64,96},{96,128},{128,160},{160,192},{192,224},{224... | collective-permute-start | bytes 294920 | tf_op jit(solution)/shard_map/while/body/eval_jaxpr/ppermute | solution.py:10
  125.5 4.1 %collective-permute-start = (bf16[64,768]{1,0:T(8,128)(2,1)S(1)}, bf16[64,768]{1,0:T(8,128)(2,1)S(1)}, u32[]{:S(2)}, u32[]{:S(2)}) collective-permute-start(bf16[64,768]{1,0:T(8,128)(2,1)S(1)} %get-tuple-element.232), channel_id=1, source_target_pairs={{0,32},{32,64},{64,96},{96,128},{128,160},{160,192},{192,224},{224... | collective-permute-start | bytes 294920 | tf_op jit(solution)/shard_map/while/body/eval_jaxpr/ppermute | solution.py:10
  130.9 4.1 %collective-permute-start = (bf16[64,768]{1,0:T(8,128)(2,1)S(1)}, bf16[64,768]{1,0:T(8,128)(2,1)S(1)}, u32[]{:S(2)}, u32[]{:S(2)}) collective-permute-start(bf16[64,768]{1,0:T(8,128)(2,1)S(1)} %get-tuple-element.232), channel_id=1, source_target_pairs={{0,32},{32,64},{64,96},{96,128},{128,160},{160,192},{192,224},{224... | collective-permute-start | bytes 294920 | tf_op jit(solution)/shard_map/while/body/eval_jaxpr/ppermute | solution.py:10
  136.3 4.1 %collective-permute-start = (bf16[64,768]{1,0:T(8,128)(2,1)S(1)}, bf16[64,768]{1,0:T(8,128)(2,1)S(1)}, u32[]{:S(2)}, u32[]{:S(2)}) collective-permute-start(bf16[64,768]{1,0:T(8,128)(2,1)S(1)} %get-tuple-element.232), channel_id=1, source_target_pairs={{0,32},{32,64},{64,96},{96,128},{128,160},{160,192},{192,224},{224... | collective-permute-start | bytes 294920 | tf_op jit(solution)/shard_map/while/body/eval_jaxpr/ppermute | solution.py:10
  141.7 4.1 %collective-permute-start = (bf16[64,768]{1,0:T(8,128)(2,1)S(1)}, bf16[64,768]{1,0:T(8,128)(2,1)S(1)}, u32[]{:S(2)}, u32[]{:S(2)}) collective-permute-start(bf16[64,768]{1,0:T(8,128)(2,1)S(1)} %get-tuple-element.232), channel_id=1, source_target_pairs={{0,32},{32,64},{64,96},{96,128},{128,160},{160,192},{192,224},{224... | collective-permute-start | bytes 294920 | tf_op jit(solution)/shard_map/while/body/eval_jaxpr/ppermute | solution.py:10
  147.2 4.6 %collective-permute-start = (bf16[64,768]{1,0:T(8,128)(2,1)S(1)}, bf16[64,768]{1,0:T(8,128)(2,1)S(1)}, u32[]{:S(2)}, u32[]{:S(2)}) collective-permute-start(bf16[64,768]{1,0:T(8,128)(2,1)S(1)} %get-tuple-element.232), channel_id=1, source_target_pairs={{0,32},{32,64},{64,96},{96,128},{128,160},{160,192},{192,224},{224... | collective-permute-start | bytes 294920 | tf_op jit(solution)/shard_map/while/body/eval_jaxpr/ppermute | solution.py:10
  153.1 5.3 %collective-permute-start = (bf16[64,768]{1,0:T(8,128)(2,1)S(1)}, bf16[64,768]{1,0:T(8,128)(2,1)S(1)}, u32[]{:S(2)}, u32[]{:S(2)}) collective-permute-start(bf16[64,768]{1,0:T(8,128)(2,1)S(1)} %get-tuple-element.232), channel_id=1, source_target_pairs={{0,32},{32,64},{64,96},{96,128},{128,160},{160,192},{192,224},{224... | collective-permute-start | bytes 294920 | tf_op jit(solution)/shard_map/while/body/eval_jaxpr/ppermute | solution.py:10
  159.7 5.3 %collective-permute-start = (bf16[64,768]{1,0:T(8,128)(2,1)S(1)}, bf16[64,768]{1,0:T(8,128)(2,1)S(1)}, u32[]{:S(2)}, u32[]{:S(2)}) collective-permute-start(bf16[64,768]{1,0:T(8,128)(2,1)S(1)} %get-tuple-element.232), channel_id=1, source_target_pairs={{0,32},{32,64},{64,96},{96,128},{128,160},{160,192},{192,224},{224... | collective-permute-start | bytes 294920 | tf_op jit(solution)/shard_map/while/body/eval_jaxpr/ppermute | solution.py:10
  166.3 5.3 %collective-permute-start = (bf16[64,768]{1,0:T(8,128)(2,1)S(1)}, bf16[64,768]{1,0:T(8,128)(2,1)S(1)}, u32[]{:S(2)}, u32[]{:S(2)}) collective-permute-start(bf16[64,768]{1,0:T(8,128)(2,1)S(1)} %get-tuple-element.232), channel_id=1, source_target_pairs={{0,32},{32,64},{64,96},{96,128},{128,160},{160,192},{192,224},{224... | collective-permute-start | bytes 294920 | tf_op jit(solution)/shard_map/while/body/eval_jaxpr/ppermute | solution.py:10
  173.0 5.3 %collective-permute-start = (bf16[64,768]{1,0:T(8,128)(2,1)S(1)}, bf16[64,768]{1,0:T(8,128)(2,1)S(1)}, u32[]{:S(2)}, u32[]{:S(2)}) collective-permute-start(bf16[64,768]{1,0:T(8,128)(2,1)S(1)} %get-tuple-element.232), channel_id=1, source_target_pairs={{0,32},{32,64},{64,96},{96,128},{128,160},{160,192},{192,224},{224... | collective-permute-start | bytes 294920 | tf_op jit(solution)/shard_map/while/body/eval_jaxpr/ppermute | solution.py:10
  179.6 5.3 %collective-permute-start = (bf16[64,768]{1,0:T(8,128)(2,1)S(1)}, bf16[64,768]{1,0:T(8,128)(2,1)S(1)}, u32[]{:S(2)}, u32[]{:S(2)}) collective-permute-start(bf16[64,768]{1,0:T(8,128)(2,1)S(1)} %get-tuple-element.232), channel_id=1, source_target_pairs={{0,32},{32,64},{64,96},{96,128},{128,160},{160,192},{192,224},{224... | collective-permute-start | bytes 294920 | tf_op jit(solution)/shard_map/while/body/eval_jaxpr/ppermute | solution.py:10
  186.2 5.3 %collective-permute-start = (bf16[64,768]{1,0:T(8,128)(2,1)S(1)}, bf16[64,768]{1,0:T(8,128)(2,1)S(1)}, u32[]{:S(2)}, u32[]{:S(2)}) collective-permute-start(bf16[64,768]{1,0:T(8,128)(2,1)S(1)} %get-tuple-element.232), channel_id=1, source_target_pairs={{0,32},{32,64},{64,96},{96,128},{128,160},{160,192},{192,224},{224... | collective-permute-start | bytes 294920 | tf_op jit(solution)/shard_map/while/body/eval_jaxpr/ppermute | solution.py:10
  192.9 5.3 %collective-permute-start = (bf16[64,768]{1,0:T(8,128)(2,1)S(1)}, bf16[64,768]{1,0:T(8,128)(2,1)S(1)}, u32[]{:S(2)}, u32[]{:S(2)}) collective-permute-start(bf16[64,768]{1,0:T(8,128)(2,1)S(1)} %get-tuple-element.232), channel_id=1, source_target_pairs={{0,32},{32,64},{64,96},{96,128},{128,160},{160,192},{192,224},{224... | collective-permute-start | bytes 294920 | tf_op jit(solution)/shard_map/while/body/eval_jaxpr/ppermute | solution.py:10
  199.5 5.3 %collective-permute-start = (bf16[64,768]{1,0:T(8,128)(2,1)S(1)}, bf16[64,768]{1,0:T(8,128)(2,1)S(1)}, u32[]{:S(2)}, u32[]{:S(2)}) collective-permute-start(bf16[64,768]{1,0:T(8,128)(2,1)S(1)} %get-tuple-element.232), channel_id=1, source_target_pairs={{0,32},{32,64},{64,96},{96,128},{128,160},{160,192},{192,224},{224... | collective-permute-start | bytes 294920 | tf_op jit(solution)/shard_map/while/body/eval_jaxpr/ppermute | solution.py:10
  206.1 5.3 %collective-permute-start = (bf16[64,768]{1,0:T(8,128)(2,1)S(1)}, bf16[64,768]{1,0:T(8,128)(2,1)S(1)}, u32[]{:S(2)}, u32[]{:S(2)}) collective-permute-start(bf16[64,768]{1,0:T(8,128)(2,1)S(1)} %get-tuple-element.232), channel_id=1, source_target_pairs={{0,32},{32,64},{64,96},{96,128},{128,160},{160,192},{192,224},{224... | collective-permute-start | bytes 294920 | tf_op jit(solution)/shard_map/while/body/eval_jaxpr/ppermute | solution.py:10
  263.4 5.5 %collective-permute-start.1 = (f32[1,2,64]{2,1,0:T(2,128)S(1)}, f32[1,2,64]{2,1,0:T(2,128)S(1)}, u32[]{:S(2)}, u32[]{:S(2)}) collective-permute-start(f32[1,2,64]{2,1,0:T(2,128)S(1)} %constant_dynamic-slice_fusion), channel_id=1, source_target_pairs={{0,1},{1,0},{2,3},{3,2},{4,5},{5,4},{6,7},{7,6},{8,9},{9,8},{10,11... | collective-permute-start | bytes 1544 | tf_op jit(solution)/shard_map/ppermute | solution.py:58
  269.5 6.4 %collective-permute-start.2 = (f32[1,2,64]{2,1,0:T(2,128)S(1)}, f32[1,2,64]{2,1,0:T(2,128)S(1)}, u32[]{:S(2)}, u32[]{:S(2)}) collective-permute-start(f32[1,2,64]{2,1,0:T(2,128)S(1)} %fusion.22), channel_id=1, source_target_pairs={{0,2},{1,3},{2,0},{3,1},{4,6},{5,7},{6,4},{7,5},{8,10},{9,11},{10,... | collective-permute-start | bytes 1544 | tf_op jit(solution)/shard_map/ppermute | solution.py:58
  275.9 9.4 %collective-permute-start.3 = (f32[1,2,64]{2,1,0:T(2,128)S(1)}, f32[1,2,64]{2,1,0:T(2,128)S(1)}, u32[]{:S(2)}, u32[]{:S(2)}) collective-permute-start(f32[1,2,64]{2,1,0:T(2,128)S(1)} %add.163), channel_id=1, source_target_pairs={{0,4},{1,5},{2,6},{3,7},{4,0},{5,1},{6,2},{7,3},{8,12},{9,13},{10,... | collective-permute-start | bytes 1544 | tf_op jit(solution)/shard_map/ppermute | solution.py:58
  285.2 5.5 %collective-permute-start.4 = (f32[1,2,64]{2,1,0:T(2,128)S(1)}, f32[1,2,64]{2,1,0:T(2,128)S(1)}, u32[]{:S(2)}, u32[]{:S(2)}) collective-permute-start(f32[1,2,64]{2,1,0:T(2,128)S(1)} %add.164), channel_id=1, source_target_pairs={{0,8},{1,9},{2,10},{3,11},{4,12},{5,13},{6,14},{7,15},{8,0},{9,1},... | collective-permute-start | bytes 1544 | tf_op jit(solution)/shard_map/ppermute | solution.py:58
  290.7 7.0 %collective-permute-start.5 = (f32[1,2,64]{2,1,0:T(2,128)S(1)}, f32[1,2,64]{2,1,0:T(2,128)S(1)}, u32[]{:S(2)}, u32[]{:S(2)}) collective-permute-start(f32[1,2,64]{2,1,0:T(2,128)S(1)} %add.165), channel_id=1, source_target_pairs={{0,16},{1,17},{2,18},{3,19},{4,20},{5,21},{6,22},{7,23},{8,24},{9,... | collective-permute-start | bytes 1544 | tf_op jit(solution)/shard_map/ppermute | solution.py:58
  (1 other events, 1.9 us)
Sparse Core Ops, SparseCore 0:
  11.2 99.2 all-gather.2
  120.1 217.1 reduce-scatter.1
